TPU v7x, 32 devices: a whole 2x2x4 slice. The times are simulated.
32 devices in a mesh: dp: 8 (over y, x, core), blk: 4 (over z).
Axes of the slice: x: 2, y: 2, z: 4, core: 2. Of those that a mesh axis runs over, the one named last changes fastest.
Arguments:
- captions: bfloat16 [512, 1152], P('dp'), may hold values from -6 to 6
- w_in: bfloat16 [1152, 4096], P(None, 'blk'), may hold values from -0.1875 to 0.1875
- w_out: bfloat16 [4096, 1152], P('blk'), may hold values from -0.09375 to 0.09375
- images: bfloat16 [128, 1152], P('blk'), may hold values from -6 to 6
- pairs: int32 [512], P('dp'), may hold values from 0 to 127
Outputs:
- grad_w_in: float32 [1152, 4096], P('dp', 'blk')
- grad_w_out_t: float32 [1152, 4096], P('dp', 'blk')
All inputs are finite; a program needn't handle non-finite values.
Results may differ from a plain program's by a relative error of at most 0.005.
Values may be sent and summed in bfloat16 or wider, within the bound.
A program may use at most 64 MiB of HBM per device.

v0:
```python
import jax
import jax.numpy as jnp
from jax import lax
from jax.sharding import PartitionSpec as P

SCORE_SCALE = 10.0
SCORE_BIAS_TERM = -5.0
EPSILON = 1e-06


def from_behind(block, axis, distance):
    devices = range(lax.axis_size(axis))
    route = [((i - distance) % len(devices), i) for i in devices]
    return lax.ppermute(block, axis, route)


def activate(values):
    return jax.nn.gelu(values, approximate=True)


def tile_grad(direction_halfway, image_direction, first_image, row_pairs):
    pair_scores = (
        SCORE_SCALE
        * lax.dot_general(
            direction_halfway,
            image_direction,
            (((1,), (1,)), ((), ())),
            preferred_element_type=jnp.float32,
        )
        + SCORE_BIAS_TERM
    )
    columns = first_image + lax.broadcasted_iota(jnp.int32, pair_scores.shape, 1)
    labels = (row_pairs[:, None] == columns).astype(jnp.float32)
    label_error = (jax.nn.sigmoid(pair_scores) - labels).astype(jnp.bfloat16)
    return SCORE_SCALE * jnp.dot(label_error, image_direction, preferred_element_type=jnp.float32)


def body(captions, w_in, w_out, images, pairs):
    cycle_size = lax.axis_size("blk")
    cycle_pos = lax.axis_index("blk")
    own_rows = captions.shape[0] // cycle_size
    block_len = images.shape[0]
    width = captions.shape[1]
    pre_act = jnp.dot(captions, w_in, preferred_element_type=jnp.float32)
    hidden = activate(pre_act).astype(jnp.bfloat16)
    rows_hidden = hidden
    embedding = lax.psum_scatter(
        jnp.dot(rows_hidden, w_out, preferred_element_type=jnp.float32),
        "blk",
        scatter_dimension=0,
        tiled=True,
    )
    inv_norm = lax.rsqrt(jnp.sum(embedding * embedding, axis=1, keepdims=True) + EPSILON)
    unit_dir = embedding * inv_norm
    direction_halfway = unit_dir.astype(jnp.bfloat16)
    image_vals = images.astype(jnp.float32)
    image_direction = (
        image_vals * lax.rsqrt(jnp.sum(image_vals * image_vals, axis=1, keepdims=True) + EPSILON)
    ).astype(jnp.bfloat16)
    row_pairs = lax.dynamic_slice_in_dim(pairs, cycle_pos * own_rows, own_rows, 0)

    def visit(step, carry):
        running, block = carry
        source = (cycle_pos - step) % cycle_size
        running = running + tile_grad(direction_halfway, block, source * block_len, row_pairs)
        block = from_behind(block, "blk", 1)
        return (running, block)

    start_sum = jnp.zeros((own_rows, width), jnp.float32)
    running, block = lax.fori_loop(0, cycle_size - 1, visit, (start_sum, image_direction))
    source = (cycle_pos - (cycle_size - 1)) % cycle_size
    direction_gradient = running + tile_grad(
        direction_halfway, block, source * block_len, row_pairs
    )
    embed_grad = (
        direction_gradient
        - unit_dir * jnp.sum(unit_dir * direction_gradient, axis=1, keepdims=True)
    ) * inv_norm
    embed_half = embed_grad.astype(jnp.bfloat16)
    piece = lax.all_gather(embed_half, "blk", axis=0, tiled=True)
    rows_hidden = hidden
    hidden_grad = lax.dot_general(
        piece, w_out, (((1,), (1,)), ((), ())), preferred_element_type=jnp.float32
    )
    _, pullback = jax.vjp(activate, pre_act)
    preact_grad = pullback(hidden_grad)[0].astype(jnp.bfloat16)
    grad_in = lax.dot_general(
        captions, preact_grad, (((0,), (0,)), ((), ())), preferred_element_type=jnp.float32
    )
    grad_out = lax.dot_general(
        piece, rows_hidden, (((0,), (0,)), ((), ())), preferred_element_type=jnp.float32
    )
    grad_in, grad_out = (grad_in, grad_out)
    grad_w_in, grad_w_out_t = (
        lax.psum_scatter(grad_in, "dp", scatter_dimension=0, tiled=True),
        lax.psum_scatter(grad_out, "dp", scatter_dimension=0, tiled=True),
    )
    return (grad_w_in, grad_w_out_t)


def solution(mesh):
    return jax.shard_map(
        body,
        mesh=mesh,
        in_specs=(P("dp", None), P(None, "blk"), P("blk", None), P("blk", None), P("dp")),
        out_specs=(P("dp", "blk"), P("dp", "blk")),
        check_vma=False,
    )
```

profile of v0, /device:TPU:0, one launch (start us, length us, event | category | flops | bytes accessed | tf_op | source)
XLA Modules:
  0.0 195.3 jit_solution(736991346852164204)
XLA Ops:
  7.2 0.0 copy-start
  7.2 0.0 reduce-scatter.6.cloned.1.call-start
  7.2 2.4 %fusion.62 = f32[64,1024]{1,0:T(8,128)S(1)} fusion(bf16[64,1152]{1,0:T(8,128)(2,1)} %param.7, bf16[1152,1024]{1,0:T(8,128)(2,1)} %param.8), kind=kOutput, calls=%fused_computation.78 | convolution fusion | flops 150994944 | bytes 2768896 | tf_op jit(solution)/shard_map/dot_general | solution.py:44
  9.7 0.0 copy-start.4
  9.7 1.2 fusion.59
  10.9 0.0 reduce-scatter.6.cloned.1.call-update
  10.9 0.0 reduce-scatter.10.cloned.1.call-start
  11.0 0.1 fusion.33
  11.2 0.1 dynamic_slice.3
  11.3 0.1 fusion.34
  11.4 22.3 %reduce-scatter.6.cloned.1.call-done = f32[16,1152]{1,0:T(8,128)} async-done(((f32[64,1152]{1,0:T(8,128)}), f32[16,1152]{1,0:T(8,128)}) %reduce-scatter.6.cloned.1.call-update) | async-done | bytes 73744 | tf_op jit(solution)/shard_map/reduce_scatter | solution.py:47
  33.7 1.1 multiply_reduce_fusion.1
  34.8 1.0 multiply_convert_fusion.2
  35.7 18.6 %while.18 = (s32[]{:T(128)}, f32[16,1152]{1,0:T(8,128)S(1)}, bf16[32,1152]{1,0:T(8,128)(2,1)S(1)}, bf16[16,1152]{1,0:T(8,128)(2,1)S(1)}, s32[16]{0:T(128)S(1)}, ...) while((s32[]{:T(128)}, f32[16,1152]{1,0:T(8,128)S(1)}, ...), condition=%wide.region_4.5_spmd.clone, body=%wide.region_3.4_spmd.clone.sunk | while | flops 2419248 | bytes 701032 | solution.py:70
  35.7 0.1 collective-permute-start
  35.8 0.3 fusion.82
  36.2 5.8 %collective-permute-done = bf16[32,1152]{1,0:T(8,128)(2,1)S(1)} collective-permute-done((bf16[32,1152]{1,0:T(8,128)(2,1)S(1)}, bf16[32,1152]{1,0:T(8,128)(2,1)S(1)}, u32[]{:S(2)}, u32[]{:S(2)}) %collective-permute-start) | collective-permute-done | bytes 73760 | tf_op jit(solution)/shard_map/while/body/eval_jaxpr/ppermute | solution.py:14
  42.0 0.3 fusion.82
  42.3 5.8 %collective-permute-done = bf16[32,1152]{1,0:T(8,128)(2,1)S(1)} collective-permute-done((bf16[32,1152]{1,0:T(8,128)(2,1)S(1)}, bf16[32,1152]{1,0:T(8,128)(2,1)S(1)}, u32[]{:S(2)}, u32[]{:S(2)}) %collective-permute-start) | collective-permute-done | bytes 73760 | tf_op jit(solution)/shard_map/while/body/eval_jaxpr/ppermute | solution.py:14
  48.2 0.3 fusion.82
  48.5 5.8 %collective-permute-done = bf16[32,1152]{1,0:T(8,128)(2,1)S(1)} collective-permute-done((bf16[32,1152]{1,0:T(8,128)(2,1)S(1)}, bf16[32,1152]{1,0:T(8,128)(2,1)S(1)}, u32[]{:S(2)}, u32[]{:S(2)}) %collective-permute-start) | collective-permute-done | bytes 73760 | tf_op jit(solution)/shard_map/while/body/eval_jaxpr/ppermute | solution.py:14
  54.3 0.5 multiply_reduce_fusion
  54.8 0.1 multiply_convert_fusion.1
  54.9 13.5 %all_gather.3 = bf16[64,1152]{1,0:T(8,128)(2,1)S(1)} all-gather(bf16[16,1152]{1,0:T(8,128)(2,1)S(1)} %multiply_convert_fusion.1), channel_id=1, replica_groups=mesh['dp'=8,'blk'=4] {'blk'}, dimensions={0}, use_global_device_ids=true | all-gather | bytes 184320 | tf_op jit(solution)/shard_map/all_gather | solution.py:80
  68.4 3.7 %convolution_bitcast_fusion = f32[1152,1024]{0,1:T(8,128)} fusion(bf16[64,1152]{1,0:T(8,128)(2,1)S(1)} %copy-done.2, f32[64,1024]{1,0:T(8,128)S(1)} %fusion.62, bf16[64,1152]{1,0:T(8,128)(2,1)S(1)} %all_gather.3, bf16[1024,1152]{1,0:T(8,128)(2,1)S(1)} %copy-done), kind=kOutput, calls=%fused_computation.21 | convolution fusion | flops 303300608 | bytes 7634944 | tf_op jit(solution)/shard_map/dot_general | solution.py:87
  72.1 6.0 %copy.9 = f32[1152,1024]{1,0:T(8,128)} copy(f32[1152,1024]{0,1:T(8,128)} %convolution_bitcast_fusion) | data formatting | bytes 9437184
  78.1 0.0 reduce-scatter.10.cloned.1.call-update
  78.2 0.0 reduce-scatter.8.cloned.1.call-start
  78.2 3.0 %fusion.58 = f32[1152,1024]{1,0:T(8,128)} fusion(bf16[64,1152]{1,0:T(8,128)(2,1)S(1)} %all_gather.3, f32[64,1024]{1,0:T(8,128)S(1)} %fusion.62), kind=kOutput, calls=%fused_computation.75 | convolution fusion | flops 151584768 | bytes 5128192 | tf_op jit(solution)/shard_map/dot_general | solution.py:90
  81.2 0.0 reduce-scatter.8.cloned.1.call-update
  81.2 49.2 %reduce-scatter.10.cloned.1.call-done = f32[144,1024]{1,0:T(8,128)} async-done(((f32[1152,1024]{1,0:T(8,128)}), f32[144,1024]{1,0:T(8,128)}) %reduce-scatter.10.cloned.1.call-update) | async-done | bytes 589840
  130.4 58.4 %reduce-scatter.8.cloned.1.call-done = f32[144,1024]{1,0:T(8,128)} async-done(((f32[1152,1024]{1,0:T(8,128)}), f32[144,1024]{1,0:T(8,128)}) %reduce-scatter.8.cloned.1.call-update) | async-done | bytes 589840 | tf_op jit(solution)/shard_map/reduce_scatter | solution.py:96
  (20 shorter events, 0.1 us)
Async XLA Ops:
  7.2 2.5 %copy-start = (bf16[1024,1152]{1,0:T(8,128)(2,1)S(1)}, bf16[1024,1152]{1,0:T(8,128)(2,1)}, u32[]{:S(2)}) copy-start(bf16[1024,1152]{1,0:T(8,128)(2,1)} %param.9) | copy-start | bytes 7077892
  7.2 3.8 %copy-start.3 = (bf16[32,1152]{1,0:T(8,128)(2,1)S(1)}, bf16[32,1152]{1,0:T(8,128)(2,1)}, u32[]{:S(2)}) copy-start(bf16[32,1152]{1,0:T(8,128)(2,1)} %param.10) | copy-start | bytes 221188
  7.2 26.5 %reduce-scatter.6.cloned.1.call-start = ((), (), s32[]{:S(2)}) async-start(), calls=%async_computation.3 | async-start | bytes 368640 | tf_op jit(solution)/shard_map/reduce_scatter | solution.py:47
  9.7 1.5 copy-start.4
  10.9 57.5 %copy-start.2 = (bf16[64,1152]{1,0:T(8,128)(2,1)S(1)}, bf16[64,1152]{1,0:T(8,128)(2,1)}, u32[]{:S(2)}) copy-start(bf16[64,1152]{1,0:T(8,128)(2,1)} %param.7) | copy-start | bytes 442372
  10.9 119.5 %reduce-scatter.10.cloned.1.call-start = ((), (), s32[]{:S(2)}) async-start(), calls=%async_computation.5 | async-start | bytes 5308416
  33.7 20.6 %copy-start.1 = (f32[16,1152]{1,0:T(8,128)S(1)}, f32[16,1152]{1,0:T(8,128)}, u32[]{:S(2)}) copy-start(f32[16,1152]{1,0:T(8,128)} %reduce-scatter.6.cloned.1.call-done) | copy-start | bytes 221188
  35.7 6.2 %collective-permute-start = (bf16[32,1152]{1,0:T(8,128)(2,1)S(1)}, bf16[32,1152]{1,0:T(8,128)(2,1)S(1)}, u32[]{:S(2)}, u32[]{:S(2)}) collective-permute-start(bf16[32,1152]{1,0:T(8,128)(2,1)S(1)} %copy.16), channel_id=1, source_target_pairs={{3,0},{0,1},{1,2},{2,3},{7,4},{4,5},{5,6},{6,7},{11,8},{8,9},{9,10... | collective-permute-start | bytes 221192 | tf_op jit(solution)/shard_map/while/body/eval_jaxpr/ppermute | solution.py:14
  42.0 6.2 %collective-permute-start = (bf16[32,1152]{1,0:T(8,128)(2,1)S(1)}, bf16[32,1152]{1,0:T(8,128)(2,1)S(1)}, u32[]{:S(2)}, u32[]{:S(2)}) collective-permute-start(bf16[32,1152]{1,0:T(8,128)(2,1)S(1)} %copy.16), channel_id=1, source_target_pairs={{3,0},{0,1},{1,2},{2,3},{7,4},{4,5},{5,6},{6,7},{11,8},{8,9},{9,10... | collective-permute-start | bytes 221192 | tf_op jit(solution)/shard_map/while/body/eval_jaxpr/ppermute | solution.py:14
  48.1 6.2 %collective-permute-start = (bf16[32,1152]{1,0:T(8,128)(2,1)S(1)}, bf16[32,1152]{1,0:T(8,128)(2,1)S(1)}, u32[]{:S(2)}, u32[]{:S(2)}) collective-permute-start(bf16[32,1152]{1,0:T(8,128)(2,1)S(1)} %copy.16), channel_id=1, source_target_pairs={{3,0},{0,1},{1,2},{2,3},{7,4},{4,5},{5,6},{6,7},{11,8},{8,9},{9,10... | collective-permute-start | bytes 221192 | tf_op jit(solution)/shard_map/while/body/eval_jaxpr/ppermute | solution.py:14
  78.2 110.6 %reduce-scatter.8.cloned.1.call-start = ((), (), s32[]{:S(2)}) async-start(), calls=%async_computation.4 | async-start | bytes 5308416 | tf_op jit(solution)/shard_map/reduce_scatter | solution.py:96
Sparse Core Ops, SparseCore 0:
  11.1 22.5 reduce-scatter.5
  78.3 52.0 reduce-scatter.9
  134.8 53.8 reduce-scatter.7
where the time goes:
time: 196 us; the launch traced here: 195 us
  waiting for transfers between devices  147 us (75%)
  between operations  13.9 us (7%)
  blocking collectives  13.5 us (7%)
  matrix products  11.8 us (6%)
  local copies, waits for them, and re-layouts  6.16 us (3%)
  other arithmetic  2.37 us (1%)
    reduce_scatter x1, waiting for transfers between devices, body(): lax.psum_scatter(grad_out, 'dp', scatter_dimension=0, tiled=True)  58.4 us
    unnamed x4, waiting for transfers between devices  49.2 us
    reduce_scatter x1, waiting for transfers between devices, body(): lax.psum_scatter(jnp.dot(rows_hidden, w_out, preferred_element_type=jnp.f...  22.3 us
    ppermute x3, waiting for transfers between devices, from_behind(): return lax.ppermute(block, axis, route)  17.4 us
    all_gather x1, blocking collectives, body(): piece = lax.all_gather(embed_half, 'blk', axis=0, tiled=True)  13.5 us
    unnamed x11, local copies, waits for them, and re-layouts  6.06 us
  transfers between devices with their start and end apart: 6, of which 6 were waited for; matrix products, arithmetic and copies ran while one was open for 2% of the time, Pallas kernels for 0%

commit v1 on v0

--- a/solution.py
+++ b/solution.py
@@ -1,6 +1,10 @@
+import functools
+
 import jax
 import jax.numpy as jnp
 from jax import lax
+from jax.experimental import pallas as pl
+from jax.experimental.pallas import tpu as pltpu
 from jax.sharding import PartitionSpec as P
 
 SCORE_SCALE = 10.0
@@ -35,7 +39,7 @@
     return SCORE_SCALE * jnp.dot(label_error, image_direction, preferred_element_type=jnp.float32)
 
 
-def body(captions, w_in, w_out, images, pairs):
+def staged_body(captions, w_in, w_out, images, pairs):
     cycle_size = lax.axis_size("blk")
     cycle_pos = lax.axis_index("blk")
     own_rows = captions.shape[0] // cycle_size
@@ -98,6 +102,318 @@
     return (grad_w_in, grad_w_out_t)
 
 
+MESH = pl.DeviceIdType.MESH
+CHUNK = 256
+VMEM_BYTES = 60 * 2**20
+GELU_SCALE = 0.7978845608028654
+GELU_CUBE = 0.044715
+NT = (((1,), (1,)), ((), ()))
+
+
+def gelu_and_slope(v):
+    square = v * v
+    t = jnp.tanh(GELU_SCALE * (v + GELU_CUBE * (square * v)))
+    half = 0.5 * (1.0 + t)
+    slope = half + (0.5 * GELU_SCALE) * v * (1.0 - t * t) * (1.0 + (3.0 * GELU_CUBE) * square)
+    return v * half, slope
+
+
+def head_kernel(
+    nd, nb,
+    caps_hbm, win_hbm, wout_hbm, img_hbm, pairs, gin_hbm, gout_hbm,
+    win, wout, img, imgu, caps, emb, part, rs_send, rs_recv, hidden, slope, pgrad,
+    pick, caps_t, emb_t, gin, gout,
+    load_sem, store_sem,
+    cap_send, cap_recv, cap_fsend, cap_frecv,
+    img_send, img_recv, img_fsend, img_frecv,
+    rs_ssem, rs_rsem,
+    ez_send, ez_recv, ex_send, ex_recv, ef_send, ef_recv,
+):
+    d = lax.axis_index("dp")
+    b = lax.axis_index("blk")
+    core = d % 2
+    chip = d // 2
+    nc = nd // 2
+    sibling = chip * 2 + (1 - core)
+    rows, width = caps_hbm.shape
+    ff = win_hbm.shape[1]
+    per = img_hbm.shape[0]
+    half = per // 2
+    piece = rows // nb
+    outs = gin.shape[0]
+
+    def z_at(k):
+        return (b + k) % nb
+
+    def z_from(k):
+        return (b + nb - k) % nb
+
+    def chip_at(k):
+        return (chip + k) % nc
+
+    def chip_from(k):
+        return (chip + nc - k) % nc
+
+    def dev_rows(dev):
+        return pl.ds(pl.multiple_of(dev * rows, rows), rows)
+
+    def chip_rows(c):
+        return pl.ds(pl.multiple_of(c * (2 * rows), 2 * rows), 2 * rows)
+
+    def piece_rows(dev, z):
+        return pl.ds(pl.multiple_of(dev * rows + z * piece, piece), piece)
+
+    def remote(src, dst, send, recv, dp, blk):
+        return pltpu.make_async_remote_copy(
+            src_ref=src, dst_ref=dst, send_sem=send, recv_sem=recv,
+            device_id=(dp, blk), device_id_type=MESH,
+        )
+
+    own = dev_rows(d)
+    loads = [
+        pltpu.make_async_copy(caps_hbm, caps.at[own], load_sem.at[0]),
+        pltpu.make_async_copy(img_hbm, img.at[pl.ds(pl.multiple_of(b * per, per), per)], load_sem.at[1]),
+        pltpu.make_async_copy(win_hbm, win, load_sem.at[2]),
+        pltpu.make_async_copy(wout_hbm, wout, load_sem.at[3]),
+    ]
+    for load in loads:
+        load.start()
+
+    barrier = pltpu.get_barrier_semaphore()
+    for k in range(1, nb):
+        pl.semaphore_signal(barrier, inc=1, device_id=(d, z_at(k)), device_id_type=MESH)
+    for k in range(1, nc):
+        pl.semaphore_signal(barrier, inc=1, device_id=(chip_at(k) * 2 + core, b), device_id_type=MESH)
+    pl.semaphore_signal(barrier, inc=1, device_id=(sibling, b), device_id_type=MESH)
+
+    columns = lax.broadcasted_iota(jnp.int32, (outs, width), 1)
+    lines = lax.broadcasted_iota(jnp.int32, (outs, width), 0)
+    pick[...] = (columns == lines + d * outs).astype(jnp.float32).astype(jnp.bfloat16)
+
+    pl.semaphore_wait(barrier, nb + nc - 1)
+
+    started = []
+    half_rows = pl.ds(pl.multiple_of(b * per + core * half, half), half)
+    loads[1].wait()
+    for k in range(1, nb):
+        started.append(remote(img.at[half_rows], img.at[half_rows], img_send.at[k], img_recv.at[k], d, z_at(k)))
+        started[-1].start()
+    loads[0].wait()
+    for k in range(1, nc):
+        started.append(
+            remote(caps.at[own], caps.at[own], cap_send.at[k], cap_recv.at[k], chip_at(k) * 2 + core, b)
+        )
+        started[-1].start()
+    started.append(remote(caps.at[own], caps.at[own], cap_fsend.at[0], cap_frecv.at[0], sibling, b))
+    started[-1].start()
+
+    def forward_rows(block):
+        @pl.loop(0, ff // CHUNK)
+        def _(j):
+            cols = pl.ds(pl.multiple_of(j * CHUNK, CHUNK), CHUNK)
+            pre = jnp.dot(caps[block, :], win[:, cols], preferred_element_type=jnp.float32)
+            h, s = gelu_and_slope(pre)
+            hidden[block, cols] = h.astype(jnp.bfloat16)
+            slope[block, cols] = s
+
+    loads[2].wait()
+    forward_rows(own)
+    loads[3].wait()
+    part[...] = jnp.dot(hidden[own, :], wout[...], preferred_element_type=jnp.float32)
+    rs_send[...] = part[...].astype(jnp.bfloat16)
+    for k in range(1, nb):
+        away = pl.ds(pl.multiple_of(z_at(k) * piece, piece), piece)
+        started.append(remote(rs_send.at[away], rs_recv.at[k], rs_ssem.at[k], rs_rsem.at[k], d, z_at(k)))
+        started[-1].start()
+
+    for k in range(1, nb):
+        came = pl.ds(pl.multiple_of(z_from(k) * per + core * half, half), half)
+        remote(img.at[came], img.at[came], img_send.at[k], img_recv.at[k], d, z_at(k)).wait_recv()
+        started.append(remote(img.at[came], img.at[came], img_fsend.at[k], img_frecv.at[k], sibling, b))
+        started[-1].start()
+    for k in range(1, nb):
+        came = pl.ds(pl.multiple_of(z_from(k) * per + (1 - core) * half, half), half)
+        remote(img.at[came], img.at[came], img_fsend.at[k], img_frecv.at[k], sibling, b).wait_recv()
+    raw = img[...].astype(jnp.float32)
+    imgu[...] = (raw * lax.rsqrt(jnp.sum(raw * raw, axis=1, keepdims=True) + EPSILON)).astype(jnp.bfloat16)
+
+    score_shape = (piece, nb * per)
+    label_col = lax.broadcasted_iota(jnp.int32, score_shape, 1)
+    label_row = lax.broadcasted_iota(jnp.int32, score_shape, 0)
+    wanted = jnp.zeros(score_shape, jnp.int32)
+    for i in range(piece):
+        wanted = jnp.where(label_row == i, pairs[b * piece + i], wanted)
+    labels = (label_col == wanted).astype(jnp.float32)
+
+    embedding = part[pl.ds(pl.multiple_of(b * piece, piece), piece), :]
+    for k in range(1, nb):
+        remote(rs_send.at[pl.ds(0, piece)], rs_recv.at[k], rs_ssem.at[k], rs_rsem.at[k], d, z_at(k)).wait_recv()
+        embedding = embedding + rs_recv[k].astype(jnp.float32)
+    inv_norm = lax.rsqrt(jnp.sum(embedding * embedding, axis=1, keepdims=True) + EPSILON)
+    unit = embedding * inv_norm
+    logits = SCORE_SCALE * lax.dot_general(
+        unit.astype(jnp.bfloat16), imgu[...], NT, preferred_element_type=jnp.float32
+    ) + SCORE_BIAS_TERM
+    mismatch = (1.0 / (1.0 + jnp.exp(-logits)) - labels).astype(jnp.bfloat16)
+    unit_grad = SCORE_SCALE * jnp.dot(mismatch, imgu[...], preferred_element_type=jnp.float32)
+    embed_grad = (unit_grad - unit * jnp.sum(unit * unit_grad, axis=1, keepdims=True)) * inv_norm
+    mine = piece_rows(d, b)
+    emb[mine, :] = embed_grad.astype(jnp.bfloat16)
+
+    def spread(z, kz):
+        src = emb.at[piece_rows(d, z)]
+        for k in range(1, nc):
+            started.append(
+                remote(src, src, ex_send.at[k, kz], ex_recv.at[k, kz], chip_at(k) * 2 + core, b)
+            )
+            started[-1].start()
+        started.append(remote(src, src, ef_send.at[0, kz], ef_recv.at[0, kz], sibling, b))
+        started[-1].start()
+
+    for k in range(1, nb):
+        started.append(remote(emb.at[mine], emb.at[mine], ez_send.at[k], ez_recv.at[k], d, z_at(k)))
+        started[-1].start()
+    spread(b, 0)
+    for kz in range(1, nb):
+        src = emb.at[piece_rows(d, z_from(kz))]
+        remote(src, src, ez_send.at[kz], ez_recv.at[kz], d, z_at(kz)).wait_recv()
+        spread(z_from(kz), kz)
+
+    for k in range(1, nc):
+        src = caps.at[dev_rows(chip_from(k) * 2 + core)]
+        remote(src, src, cap_send.at[k], cap_recv.at[k], chip_at(k) * 2 + core, b).wait_recv()
+        started.append(remote(src, src, cap_fsend.at[k], cap_frecv.at[k], sibling, b))
+        started[-1].start()
+    for k in range(nc):
+        other = caps.at[dev_rows(chip_from(k) * 2 + (1 - core))]
+        remote(other, other, cap_fsend.at[k], cap_frecv.at[k], sibling, b).wait_recv()
+        if k == 0:
+            forward_rows(dev_rows(sibling))
+        else:
+            forward_rows(chip_rows(chip_from(k)))
+        caps_t[:, chip_rows(chip_from(k))] = lax.dot_general(
+            pick[...], caps[chip_rows(chip_from(k)), :], NT, preferred_element_type=jnp.float32
+        ).astype(jnp.bfloat16)
+
+    for kz in range(nb):
+        for k in range(1, nc):
+            src = emb.at[piece_rows(chip_from(k) * 2 + core, z_from(kz))]
+            remote(src, src, ex_send.at[k, kz], ex_recv.at[k, kz], chip_at(k) * 2 + core, b).wait_recv()
+            started.append(remote(src, src, ef_send.at[k, kz], ef_recv.at[k, kz], sibling, b))
+            started[-1].start()
+    for k in range(nc):
+        for kz in range(nb):
+            src = emb.at[piece_rows(chip_from(k) * 2 + (1 - core), z_from(kz))]
+            remote(src, src, ef_send.at[k, kz], ef_recv.at[k, kz], sibling, b).wait_recv()
+        block = chip_rows(chip_from(k))
+        emb_t[:, block] = lax.dot_general(
+            pick[...], emb[block, :], NT, preferred_element_type=jnp.float32
+        ).astype(jnp.bfloat16)
+
+        @pl.loop(0, ff // CHUNK)
+        def _(j):
+            cols = pl.ds(pl.multiple_of(j * CHUNK, CHUNK), CHUNK)
+            back = lax.dot_general(emb[block, :], wout[cols, :], NT, preferred_element_type=jnp.float32)
+            pgrad[block, cols] = (back * slope[block, cols]).astype(jnp.bfloat16)
+
+    def product(left, right, out):
+        @pl.loop(0, ff // CHUNK)
+        def _(j):
+            cols = pl.ds(pl.multiple_of(j * CHUNK, CHUNK), CHUNK)
+            out[:, cols] = jnp.dot(left[...], right[:, cols], preferred_element_type=jnp.float32)
+
+    product(emb_t, hidden, gout)
+    store_out = pltpu.make_async_copy(gout, gout_hbm, store_sem.at[0])
+    store_out.start()
+    product(caps_t, pgrad, gin)
+    store_in = pltpu.make_async_copy(gin, gin_hbm, store_sem.at[1])
+    store_in.start()
+    for copy in started:
+        copy.wait_send()
+    store_out.wait()
+    store_in.wait()
+
+
+def fused_body(nd, nb, captions, w_in, w_out, images, pairs):
+    rows, width = captions.shape
+    ff = w_in.shape[1]
+    per = images.shape[0]
+    piece = rows // nb
+    outs = width // nd
+    nc = nd // 2
+    half, single = jnp.bfloat16, jnp.float32
+    dma = pltpu.SemaphoreType.DMA
+    vmem = pltpu.VMEM
+    anywhere = pl.BlockSpec(memory_space=pl.ANY)
+    return pl.pallas_call(
+        functools.partial(head_kernel, nd, nb),
+        out_shape=[jax.ShapeDtypeStruct((outs, ff), single)] * 2,
+        in_specs=[anywhere] * 4 + [pl.BlockSpec(memory_space=pltpu.SMEM)],
+        out_specs=[anywhere] * 2,
+        scratch_shapes=[
+            vmem((width, ff), half),
+            vmem((ff, width), half),
+            vmem((nb * per, width), half),
+            vmem((nb * per, width), half),
+            vmem((nd * rows, width), half),
+            vmem((nd * rows, width), half),
+            vmem((rows, width), single),
+            vmem((rows, width), half),
+            vmem((nb, piece, width), half),
+            vmem((nd * rows, ff), half),
+            vmem((nd * rows, ff), single),
+            vmem((nd * rows, ff), half),
+            vmem((outs, width), half),
+            vmem((outs, nd * rows), half),
+            vmem((outs, nd * rows), half),
+            vmem((outs, ff), single),
+            vmem((outs, ff), single),
+            dma((4,)),
+            dma((2,)),
+            dma((nc,)), dma((nc,)), dma((nc,)), dma((nc,)),
+            dma((nb,)), dma((nb,)), dma((nb,)), dma((nb,)),
+            dma((nb,)), dma((nb,)),
+            dma((nb,)), dma((nb,)),
+            dma((nc, nb)), dma((nc, nb)), dma((nc, nb)), dma((nc, nb)),
+        ],
+        compiler_params=pltpu.CompilerParams(
+            collective_id=0, has_side_effects=True, vmem_limit_bytes=VMEM_BYTES
+        ),
+    )(captions, w_in, w_out, images, pairs)
+
+
+def fits(nd, nb, captions, w_in, images):
+    rows, width = captions.shape
+    ff = w_in.shape[1]
+    per = images.shape[0]
+    scratch = (
+        4 * width * ff
+        + 4 * nb * per * width
+        + 4 * nd * rows * width
+        + 16 * rows * width
+        + 8 * nd * rows * ff
+        + 8 * (width // nd) * ff
+    )
+    return (
+        nd % 2 == 0
+        and nb > 1
+        and nd > 2
+        and ff % CHUNK == 0
+        and rows % (16 * nb) == 0
+        and (2 * rows) % 128 == 0
+        and per % 32 == 0
+        and width % (16 * nd) == 0
+        and scratch < VMEM_BYTES * 3 // 4
+    )
+
+
+def body(captions, w_in, w_out, images, pairs):
+    nd, nb = lax.axis_size("dp"), lax.axis_size("blk")
+    if fits(nd, nb, captions, w_in, images):
+        return tuple(fused_body(nd, nb, captions, w_in, w_out, images, pairs))
+    return staged_body(captions, w_in, w_out, images, pairs)
+
+
 def solution(mesh):
     return jax.shard_map(
         body,

time: 196 us -> 39.6 us (0.20)
  waiting for transfers between devices: 147 us -> 0 us
  Pallas kernels: 0 us -> 34.8 us
  blocking collectives: 13.5 us -> 0 us
  between operations: 13.9 us -> 0.64 us
  matrix products: 11.8 us -> 0 us
  other arithmetic: 2.37 us -> 0 us
  local copies, waits for them, and re-layouts: 6.16 us -> 3.86 us
    reduce_scatter x2 -> x0, waiting for transfers between devices: 80.7 us -> none  [the longest x1 58.4 us: body(): lax.psum_scatter(grad_out, 'dp', scatter_dimension=0, tiled=True)]
    unnamed x4 -> x0, waiting for transfers between devices: 49.2 us -> none
    pallas_call x0 -> x1, Pallas kernels: none -> 34.8 us  [fused_body(): pl.pallas_call(functools.partial(head_kernel, nd, nb), out_shape=[jax.Sha...]
    ppermute x3 -> x0, waiting for transfers between devices: 17.4 us -> none  [from_behind(): return lax.ppermute(block, axis, route)]
    all_gather x1 -> x0, blocking collectives: 13.5 us -> none  [body(): piece = lax.all_gather(embed_half, 'blk', axis=0, tiled=True)]
    dot_general x8 -> x0, matrix products: 11.8 us -> none  [the longest x1 3.72 us: body(): lax.dot_general(captions, preact_grad, (((0,), (0,)), ((), ())), preferre...]
    unnamed x11 -> x2, local copies, waits for them, and re-layouts: 6.06 us -> 3.86 us
  transfers between devices with their start and end apart: 6 -> 0, of which waited for: 6 -> 0; matrix products, arithmetic and copies ran while one was open for 2% -> 0% of each run, Pallas kernels for 0% -> 0%
where the time goes in v1:
time: 39.6 us; the launch traced here: 39.3 us
  Pallas kernels  34.8 us (88%)
  local copies, waits for them, and re-layouts  3.86 us (10%)
  between operations  0.64 us (2%)
    pallas_call x1, Pallas kernels, fused_body(): pl.pallas_call(functools.partial(head_kernel, nd, nb), out_shape=[jax.Sha...  34.8 us
    unnamed x2, local copies, waits for them, and re-layouts  3.86 us

profile of v1, /device:TPU:0, one launch (start us, length us, event | category | flops | bytes accessed | tf_op | source)
XLA Modules:
  0.0 39.3 jit_solution(5403368632499272196)
XLA Ops:
  0.6 34.8 %shard_map.68 = (f32[144,1024]{1,0:T(8,128)}, f32[144,1024]{1,0:T(8,128)}) custom-call(bf16[64,1152]{1,0:T(8,128)(2,1)} %caps_hbm.1, bf16[1152,1024]{1,0:T(8,128)(2,1)} %win_hbm.1, bf16[1024,1152]{1,0:T(8,128)(2,1)} %wout_hbm.1, bf16[32,1152]{1,0:T(8,128)(2,1)} %img_hbm.1, s32[64]{0:T(128)} %pairs.1), custom_call_target="tpu_custom_call" | custom-call | tf_op jit(solution)/shard_map/pallas_call | solution.py:348
  35.5 1.9 %copy.9 = f32[144,1024]{1,0:T(8,128)} copy(f32[144,1024]{1,0:T(8,128)} %get-tuple-element.4) | data formatting | bytes 1179648
  37.4 1.9 %copy.10 = f32[144,1024]{1,0:T(8,128)} copy(f32[144,1024]{1,0:T(8,128)} %get-tuple-element.5) | data formatting | bytes 1179648

commit v2 on v1

v2 whole, which is shorter than its diff:
```python
import functools

import jax
import jax.numpy as jnp
from jax import lax
from jax.experimental import pallas as pl
from jax.experimental.pallas import tpu as pltpu
from jax.sharding import PartitionSpec as P

SCORE_SCALE = 10.0
SCORE_BIAS_TERM = -5.0
EPSILON = 1e-06


def from_behind(block, axis, distance):
    devices = range(lax.axis_size(axis))
    route = [((i - distance) % len(devices), i) for i in devices]
    return lax.ppermute(block, axis, route)


def activate(values):
    return jax.nn.gelu(values, approximate=True)


def tile_grad(direction_halfway, image_direction, first_image, row_pairs):
    pair_scores = (
        SCORE_SCALE
        * lax.dot_general(
            direction_halfway,
            image_direction,
            (((1,), (1,)), ((), ())),
            preferred_element_type=jnp.float32,
        )
        + SCORE_BIAS_TERM
    )
    columns = first_image + lax.broadcasted_iota(jnp.int32, pair_scores.shape, 1)
    labels = (row_pairs[:, None] == columns).astype(jnp.float32)
    label_error = (jax.nn.sigmoid(pair_scores) - labels).astype(jnp.bfloat16)
    return SCORE_SCALE * jnp.dot(label_error, image_direction, preferred_element_type=jnp.float32)


def staged_body(captions, w_in, w_out, images, pairs):
    cycle_size = lax.axis_size("blk")
    cycle_pos = lax.axis_index("blk")
    own_rows = captions.shape[0] // cycle_size
    block_len = images.shape[0]
    width = captions.shape[1]
    pre_act = jnp.dot(captions, w_in, preferred_element_type=jnp.float32)
    hidden = activate(pre_act).astype(jnp.bfloat16)
    rows_hidden = hidden
    embedding = lax.psum_scatter(
        jnp.dot(rows_hidden, w_out, preferred_element_type=jnp.float32),
        "blk",
        scatter_dimension=0,
        tiled=True,
    )
    inv_norm = lax.rsqrt(jnp.sum(embedding * embedding, axis=1, keepdims=True) + EPSILON)
    unit_dir = embedding * inv_norm
    direction_halfway = unit_dir.astype(jnp.bfloat16)
    image_vals = images.astype(jnp.float32)
    image_direction = (
        image_vals * lax.rsqrt(jnp.sum(image_vals * image_vals, axis=1, keepdims=True) + EPSILON)
    ).astype(jnp.bfloat16)
    row_pairs = lax.dynamic_slice_in_dim(pairs, cycle_pos * own_rows, own_rows, 0)

    def visit(step, carry):
        running, block = carry
        source = (cycle_pos - step) % cycle_size
        running = running + tile_grad(direction_halfway, block, source * block_len, row_pairs)
        block = from_behind(block, "blk", 1)
        return (running, block)

    start_sum = jnp.zeros((own_rows, width), jnp.float32)
    running, block = lax.fori_loop(0, cycle_size - 1, visit, (start_sum, image_direction))
    source = (cycle_pos - (cycle_size - 1)) % cycle_size
    direction_gradient = running + tile_grad(
        direction_halfway, block, source * block_len, row_pairs
    )
    embed_grad = (
        direction_gradient
        - unit_dir * jnp.sum(unit_dir * direction_gradient, axis=1, keepdims=True)
    ) * inv_norm
    embed_half = embed_grad.astype(jnp.bfloat16)
    piece = lax.all_gather(embed_half, "blk", axis=0, tiled=True)
    rows_hidden = hidden
    hidden_grad = lax.dot_general(
        piece, w_out, (((1,), (1,)), ((), ())), preferred_element_type=jnp.float32
    )
    _, pullback = jax.vjp(activate, pre_act)
    preact_grad = pullback(hidden_grad)[0].astype(jnp.bfloat16)
    grad_in = lax.dot_general(
        captions, preact_grad, (((0,), (0,)), ((), ())), preferred_element_type=jnp.float32
    )
    grad_out = lax.dot_general(
        piece, rows_hidden, (((0,), (0,)), ((), ())), preferred_element_type=jnp.float32
    )
    grad_in, grad_out = (grad_in, grad_out)
    grad_w_in, grad_w_out_t = (
        lax.psum_scatter(grad_in, "dp", scatter_dimension=0, tiled=True),
        lax.psum_scatter(grad_out, "dp", scatter_dimension=0, tiled=True),
    )
    return (grad_w_in, grad_w_out_t)


MESH = pl.DeviceIdType.MESH
CHUNK = 256
WIDE = 512
VMEM_BYTES = 60 * 2**20
GELU_SCALE = 0.7978845608028654
GELU_CUBE = 0.044715
NT = (((1,), (1,)), ((), ()))


def gelu_and_slope(v):
    square = v * v
    t = jnp.tanh(GELU_SCALE * (v + GELU_CUBE * (square * v)))
    half = 0.5 * (1.0 + t)
    slope = half + (0.5 * GELU_SCALE) * v * (1.0 - t * t) * (1.0 + (3.0 * GELU_CUBE) * square)
    return v * half, slope


def head_kernel(
    nd, nb,
    caps_hbm, win_hbm, wout_hbm, img_hbm, pairs, hidden_hbm, pgrad_hbm, capst_hbm, embt_hbm,
    win, wout, wout_t, img, imgu, caps, emb, part, rs_send, rs_recv, hidden, slope, pgrad,
    pick, caps_t, emb_t,
    load_sem, store_sem,
    cap_send, cap_recv, cap_dsend, cap_drecv, cap_fsend, cap_frecv,
    img_send, img_recv, img_xsend, img_xrecv, img_fsend, img_frecv,
    rs_ssem, rs_rsem,
    ez_send, ez_recv, ex_send, ex_recv, ed_send, ed_recv, ef_send, ef_recv,
):
    d = lax.axis_index("dp")
    b = lax.axis_index("blk")
    core = d % 2
    chip = d // 2
    chips = (chip, chip + 1 - 2 * (chip % 2), (chip + 2) % 4, 3 - chip)
    sibling = chip * 2 + (1 - core)
    rows, width = caps_hbm.shape
    ff = win_hbm.shape[1]
    per = img_hbm.shape[0]
    half = per // 2
    piece = rows // nb

    def z_at(k):
        return (b + k) % nb

    def z_from(k):
        return (b + nb - k) % nb

    def peer(r):
        return chips[r] * 2 + core

    def other(r):
        return chips[r] * 2 + (1 - core)

    def dev_rows(dev, part=0, parts=1):
        size = rows // parts
        return pl.ds(pl.multiple_of(dev * rows + part * size, size), size)

    def chip_rows(c):
        return pl.ds(pl.multiple_of(c * (2 * rows), 2 * rows), 2 * rows)

    def piece_rows(dev, z):
        return pl.ds(pl.multiple_of(dev * rows + z * piece, piece), piece)

    def image_rows(c, side):
        return pl.ds(pl.multiple_of(z_from(c) * per + side * half, half), half)

    def remote(ref, where, send, recv, dp, blk=b):
        return pltpu.make_async_remote_copy(
            src_ref=ref.at[where], dst_ref=ref.at[where], send_sem=send, recv_sem=recv,
            device_id=(dp, blk), device_id_type=MESH,
        )

    started = []

    def send(copy):
        copy.start()
        started.append(copy)

    own = dev_rows(d)
    own_images = pl.ds(pl.multiple_of(b * per, per), per)
    loads = [
        pltpu.make_async_copy(caps_hbm, caps.at[own], load_sem.at[0]),
        pltpu.make_async_copy(win_hbm, win, load_sem.at[1]),
        pltpu.make_async_copy(wout_hbm, wout, load_sem.at[2]),
        pltpu.make_async_copy(img_hbm, img.at[own_images], load_sem.at[3]),
    ]
    for load in loads:
        load.start()

    barrier = pltpu.get_barrier_semaphore()
    for k in range(1, nb):
        pl.semaphore_signal(barrier, inc=1, device_id=(d, z_at(k)), device_id_type=MESH)
    for r in (1, 2, 3):
        pl.semaphore_signal(barrier, inc=1, device_id=(peer(r), b), device_id_type=MESH)
    pl.semaphore_signal(barrier, inc=1, device_id=(sibling, b), device_id_type=MESH)

    def forward(source, target):
        @pl.loop(0, ff // CHUNK)
        def _(j):
            cols = pl.ds(pl.multiple_of(j * CHUNK, CHUNK), CHUNK)
            pre = jnp.dot(caps[source, :], win[:, cols], preferred_element_type=jnp.float32)
            h, s = gelu_and_slope(pre)
            hidden[target, cols] = h.astype(jnp.bfloat16)
            slope[target, cols] = s

    def near(side):
        return pl.ds(pl.multiple_of(side * rows, rows), rows)

    def far(r):
        return pl.ds(r * 2 * rows, 2 * rows)

    loads[0].wait()
    loads[1].wait()
    forward(own, near(core))
    loads[2].wait()
    part[...] = jnp.dot(hidden[near(core), :], wout[...], preferred_element_type=jnp.float32)
    rs_send[...] = part[...].astype(jnp.bfloat16)
    loads[3].wait()

    pl.semaphore_wait(barrier, nb + 3)

    def rs_copy(k):
        away = pl.ds(pl.multiple_of(z_at(k) * piece, piece), piece)
        return pltpu.make_async_remote_copy(
            src_ref=rs_send.at[away], dst_ref=rs_recv.at[k], send_sem=rs_ssem.at[k],
            recv_sem=rs_rsem.at[k], device_id=(d, z_at(k)), device_id_type=MESH,
        )

    def brings(c):
        return (c > 0) & (c < nb)

    def image_z(where):
        return remote(img, where, img_send.at[0], img_recv.at[0], d, (b + chip) % nb)

    @pl.when(brings(chip))
    def _():
        image_z(image_rows(0, core)).start()

    for k in range(1, nb):
        send(rs_copy(k))
    send(remote(caps, own, cap_fsend.at[0], cap_frecv.at[0], sibling))
    for r in (1, 2):
        send(remote(caps, own, cap_send.at[r], cap_recv.at[r], peer(r)))

    columns = lax.broadcasted_iota(jnp.int32, pick.shape, 1)
    lines = lax.broadcasted_iota(jnp.int32, pick.shape, 0)
    pick[...] = (columns == lines + d * pick.shape[0]).astype(jnp.float32).astype(jnp.bfloat16)

    remote(caps, dev_rows(sibling), cap_fsend.at[0], cap_frecv.at[0], sibling).wait_recv()
    forward(dev_rows(sibling), near(1 - core))

    def image_x(r, where):
        return remote(img, where, img_xsend.at[r], img_xrecv.at[r], peer(r))

    def image_f(r, where):
        return remote(img, where, img_fsend.at[r], img_frecv.at[r], sibling)

    @pl.when(brings(chip))
    def _():
        came = image_rows(chip, core)
        image_z(came).wait_recv()
        for r in (1, 2, 3):
            image_x(r, came).start()
        image_f(0, came).start()

    @pl.loop(0, ff // CHUNK)
    def _(j):
        cols = pl.ds(pl.multiple_of(j * CHUNK, CHUNK), CHUNK)
        wout_t[:, cols] = wout[cols, :].T

    for r in (1, 2, 3):
        @pl.when(brings(chips[r]))
        def _():
            came = image_rows(chips[r], core)
            image_x(r, came).wait_recv()
            image_f(r, came).start()

    for r in (1, 2):
        remote(caps, dev_rows(peer(r)), cap_send.at[r], cap_recv.at[r], peer(r)).wait_recv()
        send(remote(caps, dev_rows(peer(r), r - 1, 2), cap_dsend.at[r - 1], cap_drecv.at[r - 1], peer(3 - r)))
        send(remote(caps, dev_rows(peer(r)), cap_fsend.at[r], cap_frecv.at[r], sibling))

    for r in range(4):
        @pl.when(brings(chips[r]))
        def _():
            image_f(r, image_rows(chips[r], 1 - core)).wait_recv()
    raw = img[...].astype(jnp.float32)
    imgu[...] = (raw * lax.rsqrt(jnp.sum(raw * raw, axis=1, keepdims=True) + EPSILON)).astype(jnp.bfloat16)

    score_shape = (piece, nb * per)
    label_col = lax.broadcasted_iota(jnp.int32, score_shape, 1)
    label_row = lax.broadcasted_iota(jnp.int32, score_shape, 0)
    wanted = jnp.zeros(score_shape, jnp.int32)
    for i in range(piece):
        wanted = jnp.where(label_row == i, pairs[b * piece + i], wanted)
    labels = (label_col == wanted).astype(jnp.float32)

    embedding = part[pl.ds(pl.multiple_of(b * piece, piece), piece), :]
    for k in range(1, nb):
        rs_copy(k).wait_recv()
        embedding = embedding + rs_recv[k].astype(jnp.float32)
    inv_norm = lax.rsqrt(jnp.sum(embedding * embedding, axis=1, keepdims=True) + EPSILON)
    unit = embedding * inv_norm
    logits = SCORE_SCALE * lax.dot_general(
        unit.astype(jnp.bfloat16), imgu[...], NT, preferred_element_type=jnp.float32
    ) + SCORE_BIAS_TERM
    mismatch = (1.0 / (1.0 + jnp.exp(-logits)) - labels).astype(jnp.bfloat16)
    unit_grad = SCORE_SCALE * jnp.dot(mismatch, imgu[...], preferred_element_type=jnp.float32)
    embed_grad = (unit_grad - unit * jnp.sum(unit * unit_grad, axis=1, keepdims=True)) * inv_norm
    mine = piece_rows(d, b)
    emb[mine, :] = embed_grad.astype(jnp.bfloat16)

    def ez_copy(kz, where):
        return remote(emb, where, ez_send.at[kz], ez_recv.at[kz], d, z_at(kz))

    def ex_copy(r, kz, dev):
        return remote(emb, piece_rows(dev, z_from(kz)), ex_send.at[r, kz], ex_recv.at[r, kz], peer(r))

    def ed_copy(kz, dev):
        over = 1 if kz < nb // 2 else 2
        return remote(emb, piece_rows(dev, z_from(kz)), ed_send.at[kz], ed_recv.at[kz], peer(3 - over))

    def ef_copy(r, kz, dev):
        return remote(emb, piece_rows(dev, z_from(kz)), ef_send.at[r, kz], ef_recv.at[r, kz], sibling)

    for kz in range(1, nb):
        send(ez_copy(kz, mine))

    def spread(kz):
        for r in (1, 2):
            send(ex_copy(r, kz, d))
        send(ef_copy(0, kz, d))

    def relay(kz):
        over = 1 if kz < nb // 2 else 2
        for r in (over, 3 - over):
            ex_copy(r, kz, peer(r)).wait_recv()
            if r == over:
                send(ed_copy(kz, peer(r)))
            send(ef_copy(r, kz, peer(r)))

    def forward_chip(r):
        if r:
            forward(chip_rows(chips[r]), far(r))
        caps_t[:, far(r)] = lax.dot_general(
            pick[...], caps[chip_rows(chips[r]), :], NT, preferred_element_type=jnp.float32
        ).astype(jnp.bfloat16)

    stores = []

    def store(src, dst):
        stores.append(pltpu.make_async_copy(src, dst, store_sem.at[len(stores)]))
        stores[-1].start()

    def backward_chip(r):
        for kz in range(nb):
            ef_copy(r, kz, other(r)).wait_recv()

        @pl.loop(0, ff // CHUNK)
        def _(j):
            cols = pl.ds(pl.multiple_of(j * CHUNK, CHUNK), CHUNK)
            back = jnp.dot(emb[chip_rows(chips[r]), :], wout_t[:, cols], preferred_element_type=jnp.float32)
            pgrad[far(r), cols] = (back * slope[far(r), cols]).astype(jnp.bfloat16)

        store(pgrad.at[far(r)], pgrad_hbm.at[far(r)])
        emb_t[:, far(r)] = lax.dot_general(
            pick[...], emb[chip_rows(chips[r]), :], NT, preferred_element_type=jnp.float32
        ).astype(jnp.bfloat16)

    spread(0)
    remote(caps, dev_rows(other(1)), cap_fsend.at[1], cap_frecv.at[1], sibling).wait_recv()
    forward_chip(1)
    for kz in range(1, nb + 1):
        if kz < nb:
            ez_copy(kz, piece_rows(d, z_from(kz))).wait_recv()
            spread(kz)
        relay(kz - 1)

    for h in (0, 1):
        across = dev_rows(peer(3), h, 2)
        remote(caps, across, cap_dsend.at[h], cap_drecv.at[h], peer(2 - h)).wait_recv()
        send(remote(caps, across, cap_fsend.at[3 + h], cap_frecv.at[3 + h], sibling))
    remote(caps, dev_rows(other(2)), cap_fsend.at[2], cap_frecv.at[2], sibling).wait_recv()
    forward_chip(0)
    forward_chip(2)
    backward_chip(0)
    for kz in range(nb):
        ed_copy(kz, peer(3)).wait_recv()
        send(ef_copy(3, kz, peer(3)))
    for h in (0, 1):
        across = dev_rows(other(3), h, 2)
        remote(caps, across, cap_fsend.at[3 + h], cap_frecv.at[3 + h], sibling).wait_recv()
    forward_chip(3)
    store(hidden, hidden_hbm)
    store(caps_t, capst_hbm)
    backward_chip(1)
    backward_chip(2)
    backward_chip(3)
    store(emb_t, embt_hbm)

    @pl.when(brings(chip))
    def _():
        image_z(image_rows(0, core)).wait_send()
        came = image_rows(chip, core)
        for r in (1, 2, 3):
            image_x(r, came).wait_send()
        image_f(0, came).wait_send()

    for r in (1, 2, 3):
        @pl.when(brings(chips[r]))
        def _():
            image_f(r, image_rows(chips[r], core)).wait_send()

    for copy in started:
        copy.wait_send()
    for copy in stores:
        copy.wait()


def product_kernel(caps_t, pgrad, emb_t, hidden, gin, gout):
    gin[...] = jnp.dot(caps_t[...], pgrad[...], preferred_element_type=jnp.float32)
    gout[...] = jnp.dot(emb_t[...], hidden[...], preferred_element_type=jnp.float32)


def fused_body(nd, nb, captions, w_in, w_out, images, pairs):
    rows, width = captions.shape
    ff = w_in.shape[1]
    per = images.shape[0]
    piece = rows // nb
    outs = width // nd
    half, single = jnp.bfloat16, jnp.float32
    dma = pltpu.SemaphoreType.DMA
    vmem = pltpu.VMEM
    anywhere = pl.BlockSpec(memory_space=pl.ANY)
    hidden, pgrad, caps_t, emb_t = pl.pallas_call(
        functools.partial(head_kernel, nd, nb),
        out_shape=[
            jax.ShapeDtypeStruct((nd * rows, ff), half),
            jax.ShapeDtypeStruct((nd * rows, ff), half),
            jax.ShapeDtypeStruct((outs, nd * rows), half),
            jax.ShapeDtypeStruct((outs, nd * rows), half),
        ],
        in_specs=[anywhere] * 4 + [pl.BlockSpec(memory_space=pltpu.SMEM)],
        out_specs=[anywhere] * 4,
        scratch_shapes=[
            vmem((width, ff), half),
            vmem((ff, width), half),
            vmem((width, ff), half),
            vmem((nb * per, width), half),
            vmem((nb * per, width), half),
            vmem((nd * rows, width), half),
            vmem((nd * rows, width), half),
            vmem((rows, width), single),
            vmem((rows, width), half),
            vmem((nb, piece, width), half),
            vmem((nd * rows, ff), half),
            vmem((nd * rows, ff), single),
            vmem((nd * rows, ff), half),
            vmem((outs, width), half),
            vmem((outs, nd * rows), half),
            vmem((outs, nd * rows), half),
            dma((4,)),
            dma((7,)),
            dma((3,)), dma((3,)), dma((2,)), dma((2,)), dma((5,)), dma((5,)),
            dma((1,)), dma((1,)), dma((4,)), dma((4,)), dma((4,)), dma((4,)),
            dma((nb,)), dma((nb,)),
            dma((nb,)), dma((nb,)), dma((3, nb)), dma((3, nb)),
            dma((nb,)), dma((nb,)), dma((4, nb)), dma((4, nb)),
        ],
        compiler_params=pltpu.CompilerParams(
            collective_id=0, has_side_effects=True, vmem_limit_bytes=VMEM_BYTES
        ),
    )(captions, w_in, w_out, images, pairs)
    left = pl.BlockSpec((outs, nd * rows), lambda j: (0, 0))
    right = pl.BlockSpec((nd * rows, WIDE), lambda j: (0, j))
    result = pl.BlockSpec((outs, WIDE), lambda j: (0, j))
    return pl.pallas_call(
        product_kernel,
        grid=(ff // WIDE,),
        out_shape=[jax.ShapeDtypeStruct((outs, ff), single)] * 2,
        in_specs=[left, right, left, right],
        out_specs=[result] * 2,
        compiler_params=pltpu.CompilerParams(vmem_limit_bytes=VMEM_BYTES),
    )(caps_t, pgrad, emb_t, hidden)


def fits(nd, nb, captions, w_in, images):
    rows, width = captions.shape
    ff = w_in.shape[1]
    per = images.shape[0]
    scratch = (
        6 * width * ff
        + 4 * nb * per * width
        + 4 * nd * rows * width
        + 16 * rows * width
        + 8 * nd * rows * ff
    )
    return (
        nd == 8
        and 1 < nb <= 4
        and ff % CHUNK == 0
        and ff % WIDE == 0
        and rows % (16 * nb) == 0
        and rows % 64 == 0
        and per % 32 == 0
        and width % (16 * nd) == 0
        and scratch < VMEM_BYTES * 3 // 4
    )


def body(captions, w_in, w_out, images, pairs):
    nd, nb = lax.axis_size("dp"), lax.axis_size("blk")
    if fits(nd, nb, captions, w_in, images):
        return tuple(fused_body(nd, nb, captions, w_in, w_out, images, pairs))
    return staged_body(captions, w_in, w_out, images, pairs)


def solution(mesh):
    return jax.shard_map(
        body,
        mesh=mesh,
        in_specs=(P("dp", None), P(None, "blk"), P("blk", None), P("blk", None), P("dp")),
        out_specs=(P("dp", "blk"), P("dp", "blk")),
        check_vma=False,
    )
```

time: 39.6 us -> 40.9 us (1.033)
  Pallas kernels: 34.8 us -> 40.1 us
  local copies, waits for them, and re-layouts: 3.86 us -> 0 us
    unnamed x2 -> x0, local copies, waits for them, and re-layouts: 3.86 us -> none
    pallas_call x0 -> x1, Pallas kernels: none -> 2.71 us  [fused_body(): pl.pallas_call(product_kernel, grid=(ff // WIDE,), out_shape=[jax.ShapeDt...]
    pallas_call x1, Pallas kernels: 34.8 us -> 37.4 us  [fused_body(): pl.pallas_call(functools.partial(head_kernel, nd, nb), out_shape=[jax.Sha...]
where the time goes in v2:
time: 40.9 us; the launch traced here: 40.7 us
  Pallas kernels  40.1 us (98%)
  between operations  0.64 us (2%)
    pallas_call x1, Pallas kernels, fused_body(): pl.pallas_call(functools.partial(head_kernel, nd, nb), out_shape=[jax.Sha...  37.4 us
    pallas_call x1, Pallas kernels, fused_body(): pl.pallas_call(product_kernel, grid=(ff // WIDE,), out_shape=[jax.ShapeDt...  2.71 us

profile of v2, /device:TPU:0, one launch (start us, length us, event | category | flops | bytes accessed | tf_op | source)
XLA Modules:
  0.0 40.7 jit_solution(7930696114813332985)
XLA Ops:
  0.6 37.4 %shard_map.68 = (bf16[512,1024]{1,0:T(8,128)(2,1)}, bf16[512,1024]{1,0:T(8,128)(2,1)}, bf16[144,512]{1,0:T(8,128)(2,1)}, bf16[144,512]{1,0:T(8,128)(2,1)}) custom-call(bf16[64,1152]{1,0:T(8,128)(2,1)} %caps_hbm.1, bf16[1152,1024]{1,0:T(8,128)(2,1)} %win_hbm.1, bf16[1024,1152]{1,0:T(8,128)(2,1)} %wout_hbm.1, bf16[32,1152]{1,0:T(8,128)(2,1)} %img_hbm.1, s32[64]{0:T(128)} %pairs.1), custom_call_target="tpu_custom_call" | custom-call | tf_op jit(solution)/shard_map/pallas_call | solution.py:438
  38.0 2.7 %shard_map.69 = (f32[144,1024]{1,0:T(8,128)}, f32[144,1024]{1,0:T(8,128)}) custom-call(bf16[144,512]{1,0:T(8,128)(2,1)} %get-tuple-element.6.caps_t, bf16[512,1024]{1,0:T(8,128)(2,1)} %get-tuple-element.7.pgrad, bf16[144,512]{1,0:T(8,128)(2,1)} %get-tuple-element.8.emb_t, bf16[512,1024]{1,0:T(8,128)(2,1)} %get-tuple-element.9.hidden), custom_call_target="tpu_custom_call" | custom-call | tf_op jit(solution)/shard_map/pallas_call | solution.py:480

commit v3 on v2

--- a/solution.py
+++ b/solution.py
@@ -125,10 +125,10 @@
     win, wout, wout_t, img, imgu, caps, emb, part, rs_send, rs_recv, hidden, slope, pgrad,
     pick, caps_t, emb_t,
     load_sem, store_sem,
-    cap_send, cap_recv, cap_dsend, cap_drecv, cap_fsend, cap_frecv,
-    img_send, img_recv, img_xsend, img_xrecv, img_fsend, img_frecv,
+    cap_send, cap_recv, cap_fsend, cap_frecv,
+    img_send, img_recv, img_fsend, img_frecv,
     rs_ssem, rs_rsem,
-    ez_send, ez_recv, ex_send, ex_recv, ed_send, ed_recv, ef_send, ef_recv,
+    ez_send, ez_recv, ea_send, ea_recv, ex_send, ex_recv, ef_send, ef_recv,
 ):
     d = lax.axis_index("dp")
     b = lax.axis_index("blk")
@@ -164,8 +164,8 @@
     def piece_rows(dev, z):
         return pl.ds(pl.multiple_of(dev * rows + z * piece, piece), piece)
 
-    def image_rows(c, side):
-        return pl.ds(pl.multiple_of(z_from(c) * per + side * half, half), half)
+    def image_rows(k, side):
+        return pl.ds(pl.multiple_of(z_from(k) * per + side * half, half), half)
 
     def remote(ref, where, send, recv, dp, blk=b):
         return pltpu.make_async_remote_copy(
@@ -229,20 +229,18 @@
             recv_sem=rs_rsem.at[k], device_id=(d, z_at(k)), device_id_type=MESH,
         )
 
-    def brings(c):
-        return (c > 0) & (c < nb)
-
-    def image_z(where):
-        return remote(img, where, img_send.at[0], img_recv.at[0], d, (b + chip) % nb)
-
-    @pl.when(brings(chip))
-    def _():
-        image_z(image_rows(0, core)).start()
+    def image_z(k, where):
+        return remote(img, where, img_send.at[k], img_recv.at[k], d, z_at(k))
+
+    def image_f(k, where):
+        return remote(img, where, img_fsend.at[k], img_frecv.at[k], sibling)
 
     for k in range(1, nb):
         send(rs_copy(k))
+    for k in range(1, nb):
+        send(image_z(k, image_rows(0, core)))
     send(remote(caps, own, cap_fsend.at[0], cap_frecv.at[0], sibling))
-    for r in (1, 2):
+    for r in (1, 2, 3):
         send(remote(caps, own, cap_send.at[r], cap_recv.at[r], peer(r)))
 
     columns = lax.broadcasted_iota(jnp.int32, pick.shape, 1)
@@ -251,42 +249,18 @@
 
     remote(caps, dev_rows(sibling), cap_fsend.at[0], cap_frecv.at[0], sibling).wait_recv()
     forward(dev_rows(sibling), near(1 - core))
-
-    def image_x(r, where):
-        return remote(img, where, img_xsend.at[r], img_xrecv.at[r], peer(r))
-
-    def image_f(r, where):
-        return remote(img, where, img_fsend.at[r], img_frecv.at[r], sibling)
-
-    @pl.when(brings(chip))
-    def _():
-        came = image_rows(chip, core)
-        image_z(came).wait_recv()
-        for r in (1, 2, 3):
-            image_x(r, came).start()
-        image_f(0, came).start()
 
     @pl.loop(0, ff // CHUNK)
     def _(j):
         cols = pl.ds(pl.multiple_of(j * CHUNK, CHUNK), CHUNK)
         wout_t[:, cols] = wout[cols, :].T
 
-    for r in (1, 2, 3):
-        @pl.when(brings(chips[r]))
-        def _():
-            came = image_rows(chips[r], core)
-            image_x(r, came).wait_recv()
-            image_f(r, came).start()
-
-    for r in (1, 2):
-        remote(caps, dev_rows(peer(r)), cap_send.at[r], cap_recv.at[r], peer(r)).wait_recv()
-        send(remote(caps, dev_rows(peer(r), r - 1, 2), cap_dsend.at[r - 1], cap_drecv.at[r - 1], peer(3 - r)))
-        send(remote(caps, dev_rows(peer(r)), cap_fsend.at[r], cap_frecv.at[r], sibling))
-
-    for r in range(4):
-        @pl.when(brings(chips[r]))
-        def _():
-            image_f(r, image_rows(chips[r], 1 - core)).wait_recv()
+    for k in range(1, nb):
+        came = image_rows(k, core)
+        image_z(k, came).wait_recv()
+        send(image_f(k, came))
+    for k in range(1, nb):
+        image_f(k, image_rows(k, 1 - core)).wait_recv()
     raw = img[...].astype(jnp.float32)
     imgu[...] = (raw * lax.rsqrt(jnp.sum(raw * raw, axis=1, keepdims=True) + EPSILON)).astype(jnp.bfloat16)
 
@@ -319,9 +293,8 @@
     def ex_copy(r, kz, dev):
         return remote(emb, piece_rows(dev, z_from(kz)), ex_send.at[r, kz], ex_recv.at[r, kz], peer(r))
 
-    def ed_copy(kz, dev):
-        over = 1 if kz < nb // 2 else 2
-        return remote(emb, piece_rows(dev, z_from(kz)), ed_send.at[kz], ed_recv.at[kz], peer(3 - over))
+    def ea_copy(k, z):
+        return remote(emb, piece_rows(peer(3), z), ea_send.at[k], ea_recv.at[k], d, z_at(k))
 
     def ef_copy(r, kz, dev):
         return remote(emb, piece_rows(dev, z_from(kz)), ef_send.at[r, kz], ef_recv.at[r, kz], sibling)
@@ -329,18 +302,9 @@
     for kz in range(1, nb):
         send(ez_copy(kz, mine))
 
-    def spread(kz):
-        for r in (1, 2):
-            send(ex_copy(r, kz, d))
-        send(ef_copy(0, kz, d))
-
-    def relay(kz):
-        over = 1 if kz < nb // 2 else 2
-        for r in (over, 3 - over):
-            ex_copy(r, kz, peer(r)).wait_recv()
-            if r == over:
-                send(ed_copy(kz, peer(r)))
-            send(ef_copy(r, kz, peer(r)))
+    def forward_on(r, kz):
+        ex_copy(r, kz, peer(r)).wait_recv()
+        send(ef_copy(r, kz, peer(r)))
 
     def forward_chip(r):
         if r:
@@ -370,49 +334,49 @@
             pick[...], emb[chip_rows(chips[r]), :], NT, preferred_element_type=jnp.float32
         ).astype(jnp.bfloat16)
 
-    spread(0)
-    remote(caps, dev_rows(other(1)), cap_fsend.at[1], cap_frecv.at[1], sibling).wait_recv()
+    for r in (3, 1, 2):
+        send(ex_copy(r, 0, d))
+    send(ef_copy(0, 0, d))
+
+    for r in (1, 2, 3):
+        remote(caps, dev_rows(peer(r)), cap_send.at[r], cap_recv.at[r], peer(r)).wait_recv()
+        send(remote(caps, dev_rows(peer(r)), cap_fsend.at[r], cap_frecv.at[r], sibling))
+    forward_chip(0)
+
+    for kz in range(1, nb):
+        ez_copy(kz, piece_rows(d, z_from(kz))).wait_recv()
+        for r in (1, 2):
+            send(ex_copy(r, kz, d))
+        send(ef_copy(0, kz, d))
+        if kz == 1:
+            forward_on(3, 0)
+            for k in range(1, nb):
+                send(ea_copy(k, b))
+    for r in (1, 2):
+        forward_on(r, 0)
+
+    def caption_wait(r):
+        remote(caps, dev_rows(other(r)), cap_fsend.at[r], cap_frecv.at[r], sibling).wait_recv()
+
+    caption_wait(1)
     forward_chip(1)
-    for kz in range(1, nb + 1):
-        if kz < nb:
-            ez_copy(kz, piece_rows(d, z_from(kz))).wait_recv()
-            spread(kz)
-        relay(kz - 1)
-
-    for h in (0, 1):
-        across = dev_rows(peer(3), h, 2)
-        remote(caps, across, cap_dsend.at[h], cap_drecv.at[h], peer(2 - h)).wait_recv()
-        send(remote(caps, across, cap_fsend.at[3 + h], cap_frecv.at[3 + h], sibling))
-    remote(caps, dev_rows(other(2)), cap_fsend.at[2], cap_frecv.at[2], sibling).wait_recv()
-    forward_chip(0)
+    for kz in range(1, nb):
+        for r in (1, 2):
+            forward_on(r, kz)
+    caption_wait(2)
     forward_chip(2)
-    backward_chip(0)
-    for kz in range(nb):
-        ed_copy(kz, peer(3)).wait_recv()
+    for kz in range(1, nb):
+        ea_copy(kz, z_from(kz)).wait_recv()
         send(ef_copy(3, kz, peer(3)))
-    for h in (0, 1):
-        across = dev_rows(other(3), h, 2)
-        remote(caps, across, cap_fsend.at[3 + h], cap_frecv.at[3 + h], sibling).wait_recv()
+    caption_wait(3)
     forward_chip(3)
     store(hidden, hidden_hbm)
     store(caps_t, capst_hbm)
+    backward_chip(0)
     backward_chip(1)
     backward_chip(2)
     backward_chip(3)
     store(emb_t, embt_hbm)
-
-    @pl.when(brings(chip))
-    def _():
-        image_z(image_rows(0, core)).wait_send()
-        came = image_rows(chip, core)
-        for r in (1, 2, 3):
-            image_x(r, came).wait_send()
-        image_f(0, came).wait_send()
-
-    for r in (1, 2, 3):
-        @pl.when(brings(chips[r]))
-        def _():
-            image_f(r, image_rows(chips[r], core)).wait_send()
 
     for copy in started:
         copy.wait_send()
@@ -464,11 +428,11 @@
             vmem((outs, nd * rows), half),
             dma((4,)),
             dma((7,)),
-            dma((3,)), dma((3,)), dma((2,)), dma((2,)), dma((5,)), dma((5,)),
-            dma((1,)), dma((1,)), dma((4,)), dma((4,)), dma((4,)), dma((4,)),
+            dma((4,)), dma((4,)), dma((4,)), dma((4,)),
+            dma((nb,)), dma((nb,)), dma((nb,)), dma((nb,)),
             dma((nb,)), dma((nb,)),
-            dma((nb,)), dma((nb,)), dma((3, nb)), dma((3, nb)),
-            dma((nb,)), dma((nb,)), dma((4, nb)), dma((4, nb)),
+            dma((nb,)), dma((nb,)), dma((nb,)), dma((nb,)),
+            dma((4, nb)), dma((4, nb)), dma((4, nb)), dma((4, nb)),
         ],
         compiler_params=pltpu.CompilerParams(
             collective_id=0, has_side_effects=True, vmem_limit_bytes=VMEM_BYTES

time: 40.9 us -> 38.7 us (0.946)
  Pallas kernels: 40.1 us -> 37.9 us
    pallas_call x1, Pallas kernels: 37.4 us -> 35.2 us  [fused_body(): pl.pallas_call(functools.partial(head_kernel, nd, nb), out_shape=[jax.Sha...]
where the time goes in v3:
time: 38.7 us; the launch traced here: 38.6 us
  Pallas kernels  37.9 us (98%)
  between operations  0.64 us (2%)
    pallas_call x1, Pallas kernels, fused_body(): pl.pallas_call(functools.partial(head_kernel, nd, nb), out_shape=[jax.Sha...  35.2 us
    pallas_call x1, Pallas kernels, fused_body(): pl.pallas_call(product_kernel, grid=(ff // WIDE,), out_shape=[jax.ShapeDt...  2.71 us

profile of v3, /device:TPU:0, one launch (start us, length us, event | category | flops | bytes accessed | tf_op | source)
XLA Modules:
  0.0 38.6 jit_solution(1430942983519303985)
XLA Ops:
  0.6 35.2 %shard_map.68 = (bf16[512,1024]{1,0:T(8,128)(2,1)}, bf16[512,1024]{1,0:T(8,128)(2,1)}, bf16[144,512]{1,0:T(8,128)(2,1)}, bf16[144,512]{1,0:T(8,128)(2,1)}) custom-call(bf16[64,1152]{1,0:T(8,128)(2,1)} %caps_hbm.1, bf16[1152,1024]{1,0:T(8,128)(2,1)} %win_hbm.1, bf16[1024,1152]{1,0:T(8,128)(2,1)} %wout_hbm.1, bf16[32,1152]{1,0:T(8,128)(2,1)} %img_hbm.1, s32[64]{0:T(128)} %pairs.1), custom_call_target="tpu_custom_call" | custom-call | tf_op jit(solution)/shard_map/pallas_call | solution.py:402
  35.9 2.7 %shard_map.69 = (f32[144,1024]{1,0:T(8,128)}, f32[144,1024]{1,0:T(8,128)}) custom-call(bf16[144,512]{1,0:T(8,128)(2,1)} %get-tuple-element.6.caps_t, bf16[512,1024]{1,0:T(8,128)(2,1)} %get-tuple-element.7.pgrad, bf16[144,512]{1,0:T(8,128)(2,1)} %get-tuple-element.8.emb_t, bf16[512,1024]{1,0:T(8,128)(2,1)} %get-tuple-element.9.hidden), custom_call_target="tpu_custom_call" | custom-call | tf_op jit(solution)/shard_map/pallas_call | solution.py:444

commit v4 on v3

--- a/solution.py
+++ b/solution.py
@@ -358,22 +358,21 @@
     def caption_wait(r):
         remote(caps, dev_rows(other(r)), cap_fsend.at[r], cap_frecv.at[r], sibling).wait_recv()
 
-    caption_wait(1)
-    forward_chip(1)
+    for r in (1, 2):
+        caption_wait(r)
+        forward_chip(r)
+    backward_chip(0)
     for kz in range(1, nb):
         for r in (1, 2):
             forward_on(r, kz)
-    caption_wait(2)
-    forward_chip(2)
-    for kz in range(1, nb):
-        ea_copy(kz, z_from(kz)).wait_recv()
-        send(ef_copy(3, kz, peer(3)))
     caption_wait(3)
     forward_chip(3)
     store(hidden, hidden_hbm)
     store(caps_t, capst_hbm)
-    backward_chip(0)
     backward_chip(1)
+    for kz in range(1, nb):
+        ea_copy(kz, z_from(kz)).wait_recv()
+        send(ef_copy(3, kz, peer(3)))
     backward_chip(2)
     backward_chip(3)
     store(emb_t, embt_hbm)

time: 38.7 us -> 35.8 us (0.925)
  Pallas kernels: 37.9 us -> 35 us
    pallas_call x1, Pallas kernels: 35.2 us -> 32.3 us  [fused_body(): pl.pallas_call(functools.partial(head_kernel, nd, nb), out_shape=[jax.Sha...]
where the time goes in v4:
time: 35.8 us; the launch traced here: 35.7 us
  Pallas kernels  35 us (98%)
  between operations  0.64 us (2%)
    pallas_call x1, Pallas kernels, fused_body(): pl.pallas_call(functools.partial(head_kernel, nd, nb), out_shape=[jax.Sha...  32.3 us
    pallas_call x1, Pallas kernels, fused_body(): pl.pallas_call(product_kernel, grid=(ff // WIDE,), out_shape=[jax.ShapeDt...  2.71 us

profile of v4, /device:TPU:0, one launch (start us, length us, event | category | flops | bytes accessed | tf_op | source)
XLA Modules:
  0.0 35.7 jit_solution(12513221192768144134)
XLA Ops:
  0.6 32.3 %shard_map.68 = (bf16[512,1024]{1,0:T(8,128)(2,1)}, bf16[512,1024]{1,0:T(8,128)(2,1)}, bf16[144,512]{1,0:T(8,128)(2,1)}, bf16[144,512]{1,0:T(8,128)(2,1)}) custom-call(bf16[64,1152]{1,0:T(8,128)(2,1)} %caps_hbm.1, bf16[1152,1024]{1,0:T(8,128)(2,1)} %win_hbm.1, bf16[1024,1152]{1,0:T(8,128)(2,1)} %wout_hbm.1, bf16[32,1152]{1,0:T(8,128)(2,1)} %img_hbm.1, s32[64]{0:T(128)} %pairs.1), custom_call_target="tpu_custom_call" | custom-call | tf_op jit(solution)/shard_map/pallas_call | solution.py:401
  33.0 2.7 %shard_map.69 = (f32[144,1024]{1,0:T(8,128)}, f32[144,1024]{1,0:T(8,128)}) custom-call(bf16[144,512]{1,0:T(8,128)(2,1)} %get-tuple-element.6.caps_t, bf16[512,1024]{1,0:T(8,128)(2,1)} %get-tuple-element.7.pgrad, bf16[144,512]{1,0:T(8,128)(2,1)} %get-tuple-element.8.emb_t, bf16[512,1024]{1,0:T(8,128)(2,1)} %get-tuple-element.9.hidden), custom_call_target="tpu_custom_call" | custom-call | tf_op jit(solution)/shard_map/pallas_call | solution.py:443
